TPU v7x, 256 devices: a whole 4x4x8 slice. The times are simulated.
256 devices in a mesh: replica: 32 (over x_lo, z, core), tensor: 8 (over x_hi, y).
Axes of the slice: x: 4 (x_hi: 2, x_lo: 2; x = x_hi * 2 + x_lo), y: 4, z: 8, core: 2. Of those that a mesh axis runs over, the one named last changes fastest.
Arguments:
- context: bfloat16 [32, 2048, 1792], P('replica', None, 'tensor'), may hold values from -6 to 6
- out_grad: bfloat16 [32, 2048, 3584], P('replica', 'tensor'), may hold values from -6 to 6
- params: float32 [32, 1792, 3584], P('replica', 'tensor'), may hold values from -6 to 6
- momentum: bfloat16 [32, 1792, 3584], P('replica', 'tensor'), may hold values from -180 to 180
Outputs:
- mixed_params: float32 [32, 1792, 3584], P('replica', 'tensor')
- mixed_momentum: bfloat16 [32, 1792, 3584], P('replica', 'tensor')
All inputs are finite; a program needn't handle non-finite values.
Results may differ from a plain program's by a relative error of at most 0.0052.
Values may be sent and summed in bfloat16 or wider, within the bound.
No kernel may reach another device: no remote copies, remote signals or barrier semaphores. Data moves between devices by JAX's collectives and lax.ppermute only.
A program may use at most 128 MiB of HBM per device.

v0:
```python
import jax
import jax.numpy as jnp
from jax import lax
from jax.sharding import PartitionSpec as P

learn_rate = 0.01
beta_decay = 0.9


def passed_along(value, axis, steps):
    count = lax.axis_size(axis)
    pairs = [(source, (source + steps) % count) for source in range(count)]
    return lax.ppermute(value, axis, pairs)


def blend(own, below, above):
    return (own + below.astype(jnp.float32) + above.astype(jnp.float32)) / 3.0


def body(context, out_grad, params, momentum):
    local_ctx = context[0]
    gathered = lax.all_gather(out_grad, "tensor", axis=1, tiled=True)
    grad = lax.dot_general(
        local_ctx, gathered[0], (((0,), (0,)), ((), ())), preferred_element_type=jnp.float32
    )
    velocity = beta_decay * momentum[0].astype(jnp.float32) + grad
    stepped = params[0] - learn_rate * velocity
    step_sent = stepped.astype(jnp.bfloat16)
    vel_sent = velocity.astype(jnp.bfloat16)
    lower_one = passed_along((step_sent, vel_sent), "replica", 1)
    upper_one = passed_along((step_sent, vel_sent), "replica", -1)
    params_one = blend(stepped, lower_one[0], upper_one[0])
    velocity_one = blend(velocity, lower_one[1], upper_one[1])
    param_sent = params_one.astype(jnp.bfloat16)
    speed_sent = velocity_one.astype(jnp.bfloat16)
    lower_two = passed_along((param_sent, speed_sent), "replica", 2)
    upper_two = passed_along((param_sent, speed_sent), "replica", -2)
    params_two = blend(params_one, lower_two[0], upper_two[0])
    velocity_two = blend(velocity_one, lower_two[1], upper_two[1])
    return (params_two[None], velocity_two.astype(jnp.bfloat16)[None])


def solution(mesh):
    return jax.shard_map(
        body,
        mesh=mesh,
        in_specs=(
            P("replica", None, "tensor"),
            P("replica", "tensor", None),
            P("replica", "tensor", None),
            P("replica", "tensor", None),
        ),
        out_specs=(P("replica", "tensor", None), P("replica", "tensor", None)),
        check_vma=False,
    )
```

profile of v0, /device:TPU:1, one launch (start us, length us, event | category | flops | bytes accessed | tf_op | source)
XLA Modules:
  0.0 320.8 jit_solution(2887409313065282749)
XLA Ops:
  7.2 0.0 copy-start
  7.2 0.0 all-gather.2.cloned.1.call-start
  7.2 0.7 all-gather.2.cloned.1.call-update
  7.9 175.0 %all-gather.2.cloned.1.call-done = bf16[1,2048,3584]{2,1,0:T(8,128)(2,1)} async-done(((bf16[1,256,3584]{2,1,0:T(8,128)(2,1)}), bf16[1,2048,3584]{2,1,0:T(8,128)(2,1)}) %all-gather.2.cloned.1.call-update) | async-done | bytes 14680080 | tf_op jit(solution)/shard_map/all_gather | solution.py:22
  182.9 0.0 copy-done
  182.9 0.0 copy-start.1
  182.9 10.3 %fusion.10 = (bf16[224,3584]{1,0:T(8,128)(2,1)S(1)}, bf16[224,3584]{1,0:T(8,128)(2,1)S(1)}, f32[224,3584]{1,0:T(8,128)S(1)}) fusion(f32[1,224,3584]{2,1,0:T(8,128)} %param.6, bf16[1,2048,3584]{2,1,0:T(8,128)(2,1)} %all-gather.2.cloned.1.call-done, bf16[1,2048,224]{1,2,0:T(8,128)(2,1)S(1)} %copy-done, bf16[1,224,3584]{2,1,0:T(8,128)(2,1)} %param.7), kind=kOutput, calls=%fused_computation.13 | convolution fusion | flops 3293954048 | bytes 26836992 | tf_op jit(solution)/shard_map/dot_general | solution.py:23
  193.3 1.2 collective-permute-start.5
  194.4 1.2 collective-permute-start.4
  195.7 1.1 collective-permute-start.1
  196.8 0.6 collective-permute-start
  197.4 16.9 %collective-permute-done.5 = bf16[224,3584]{1,0:T(8,128)(2,1)S(1)} collective-permute-done((bf16[224,3584]{1,0:T(8,128)(2,1)S(1)}, bf16[224,3584]{1,0:T(8,128)(2,1)S(1)}, u32[]{:S(2)}, u32[]{:S(2)}) %collective-permute-start.5) | collective-permute-done | bytes 1605664 | tf_op jit(solution)/shard_map/ppermute | solution.py:13
  214.4 0.0 collective-permute-done.4
  214.4 17.2 %collective-permute-done.1 = bf16[224,3584]{1,0:T(8,128)(2,1)S(1)} collective-permute-done((bf16[224,3584]{1,0:T(8,128)(2,1)S(1)}, bf16[224,3584]{1,0:T(8,128)(2,1)S(1)}, u32[]{:S(2)}, u32[]{:S(2)}) %collective-permute-start.1) | collective-permute-done | bytes 1605664 | tf_op jit(solution)/shard_map/ppermute | solution.py:13
  231.6 0.0 collective-permute-done
  231.6 0.0 copy-done.1
  231.6 1.4 fusion.7
  233.0 4.4 %collective-permute-start.7 = (bf16[224,3584]{1,0:T(8,128)(2,1)S(1)}, bf16[224,3584]{1,0:T(8,128)(2,1)S(1)}, u32[]{:S(2)}, u32[]{:S(2)}) collective-permute-start(bf16[224,3584]{1,0:T(8,128)(2,1)S(1)} %get-tuple-element.4), channel_id=1, source_target_pairs={{0,240},{8,248},{16,0},{24,8},{32,16},{40,24},{48,32},{56,40},{64,... | collective-permute-start | bytes 4816904 | tf_op jit(solution)/shard_map/ppermute | solution.py:13
  237.4 0.0 collective-permute-start.6
  237.5 3.6 %collective-permute-start.3 = (bf16[224,3584]{1,0:T(8,128)(2,1)S(1)}, bf16[224,3584]{1,0:T(8,128)(2,1)S(1)}, u32[]{:S(2)}, u32[]{:S(2)}) collective-permute-start(bf16[224,3584]{1,0:T(8,128)(2,1)S(1)} %get-tuple-element.5), channel_id=1, source_target_pairs={{0,240},{8,248},{16,0},{24,8},{32,16},{40,24},{48,32},{56,40},{64,... | collective-permute-start | bytes 4816904 | tf_op jit(solution)/shard_map/ppermute | solution.py:13
  241.0 0.0 collective-permute-start.2
  241.0 30.8 %collective-permute-done.7 = bf16[224,3584]{1,0:T(8,128)(2,1)S(1)} collective-permute-done((bf16[224,3584]{1,0:T(8,128)(2,1)S(1)}, bf16[224,3584]{1,0:T(8,128)(2,1)S(1)}, u32[]{:S(2)}, u32[]{:S(2)}) %collective-permute-start.7) | collective-permute-done | bytes 1605664 | tf_op jit(solution)/shard_map/ppermute | solution.py:13
  271.8 3.9 %collective-permute-done.6 = bf16[224,3584]{1,0:T(8,128)(2,1)S(1)} collective-permute-done((bf16[224,3584]{1,0:T(8,128)(2,1)S(1)}, bf16[224,3584]{1,0:T(8,128)(2,1)S(1)}, u32[]{:S(2)}, u32[]{:S(2)}) %collective-permute-start.6) | collective-permute-done | bytes 1605664 | tf_op jit(solution)/shard_map/ppermute | solution.py:13
  275.7 30.5 %collective-permute-done.3 = bf16[224,3584]{1,0:T(8,128)(2,1)S(1)} collective-permute-done((bf16[224,3584]{1,0:T(8,128)(2,1)S(1)}, bf16[224,3584]{1,0:T(8,128)(2,1)S(1)}, u32[]{:S(2)}, u32[]{:S(2)}) %collective-permute-start.3) | collective-permute-done | bytes 1605664 | tf_op jit(solution)/shard_map/ppermute | solution.py:13
  306.3 3.9 %collective-permute-done.2 = bf16[224,3584]{1,0:T(8,128)(2,1)S(1)} collective-permute-done((bf16[224,3584]{1,0:T(8,128)(2,1)S(1)}, bf16[224,3584]{1,0:T(8,128)(2,1)S(1)}, u32[]{:S(2)}, u32[]{:S(2)}) %collective-permute-start.2) | collective-permute-done | bytes 1605664 | tf_op jit(solution)/shard_map/ppermute | solution.py:13
  310.1 3.8 %fusion.5 = (bf16[1,224,3584]{2,1,0:T(8,128)(2,1)}, f32[1,224,3584]{2,1,0:T(8,128)}) fusion(bf16[224,3584]{1,0:T(8,128)(2,1)S(1)} %collective-permute-done.7, bf16[224,3584]{1,0:T(8,128)(2,1)S(1)} %collective-permute-done.6, bf16[224,3584]{1,0:T(8,128)(2,1)S(1)} %collective-permute-done.5, f32[224,3584]{1,0:T(8,128)S(1)} %get-tuple-element.8, ...), kind=kLoop, calls=%fused_computation.8 | loop fusion | flops 18464768 | bytes 24084480 | tf_op jit(solution)/shard_map/broadcast_in_dim | solution.py:40
Async XLA Ops:
  7.2 175.8 %copy-start = (bf16[1,2048,224]{1,2,0:T(8,128)(2,1)S(1)}, bf16[1,2048,224]{1,2,0:T(8,128)(2,1)}, u32[]{:S(2)}) copy-start(bf16[1,2048,224]{1,2,0:T(8,128)(2,1)} %param.4) | copy-start | bytes 2752516
  7.2 175.8 %all-gather.2.cloned.1.call-start = ((), (), s32[]{:S(2)}) async-start(), calls=%async_computation | async-start | bytes 16515072 | tf_op jit(solution)/shard_map/all_gather | solution.py:22
  182.9 48.6 %copy-start.1 = (f32[1,224,3584]{2,1,0:T(8,128)S(1)}, f32[1,224,3584]{2,1,0:T(8,128)}, u32[]{:S(2)}) copy-start(f32[1,224,3584]{2,1,0:T(8,128)} %param.6) | copy-start | bytes 9633796
  193.3 21.1 %collective-permute-start.5 = (bf16[224,3584]{1,0:T(8,128)(2,1)S(1)}, bf16[224,3584]{1,0:T(8,128)(2,1)S(1)}, u32[]{:S(2)}, u32[]{:S(2)}) collective-permute-start(bf16[224,3584]{1,0:T(8,128)(2,1)S(1)} %get-tuple-element.6), channel_id=1, source_target_pairs={{0,248},{8,0},{16,8},{24,16},{32,24},{40,32},{48,40},{56,48},{64,5... | collective-permute-start | bytes 4816904 | tf_op jit(solution)/shard_map/ppermute | solution.py:13
  194.4 19.9 %collective-permute-start.4 = (bf16[224,3584]{1,0:T(8,128)(2,1)S(1)}, bf16[224,3584]{1,0:T(8,128)(2,1)S(1)}, u32[]{:S(2)}, u32[]{:S(2)}) collective-permute-start(bf16[224,3584]{1,0:T(8,128)(2,1)S(1)} %get-tuple-element.6), channel_id=1, source_target_pairs={{0,8},{8,16},{16,24},{24,32},{32,40},{40,48},{48,56},{56,64},{64,7... | collective-permute-start | bytes 4816904 | tf_op jit(solution)/shard_map/ppermute | solution.py:13
  195.7 35.9 %collective-permute-start.1 = (bf16[224,3584]{1,0:T(8,128)(2,1)S(1)}, bf16[224,3584]{1,0:T(8,128)(2,1)S(1)}, u32[]{:S(2)}, u32[]{:S(2)}) collective-permute-start(bf16[224,3584]{1,0:T(8,128)(2,1)S(1)} %get-tuple-element.7), channel_id=1, source_target_pairs={{0,248},{8,0},{16,8},{24,16},{32,24},{40,32},{48,40},{56,48},{64,5... | collective-permute-start | bytes 4816904 | tf_op jit(solution)/shard_map/ppermute | solution.py:13
  196.8 34.8 %collective-permute-start = (bf16[224,3584]{1,0:T(8,128)(2,1)S(1)}, bf16[224,3584]{1,0:T(8,128)(2,1)S(1)}, u32[]{:S(2)}, u32[]{:S(2)}) collective-permute-start(bf16[224,3584]{1,0:T(8,128)(2,1)S(1)} %get-tuple-element.7), channel_id=1, source_target_pairs={{0,8},{8,16},{16,24},{24,32},{32,40},{40,48},{48,56},{56,64},{64,7... | collective-permute-start | bytes 4816904 | tf_op jit(solution)/shard_map/ppermute | solution.py:13
  233.0 38.8 %collective-permute-start.7 = (bf16[224,3584]{1,0:T(8,128)(2,1)S(1)}, bf16[224,3584]{1,0:T(8,128)(2,1)S(1)}, u32[]{:S(2)}, u32[]{:S(2)}) collective-permute-start(bf16[224,3584]{1,0:T(8,128)(2,1)S(1)} %get-tuple-element.4), channel_id=1, source_target_pairs={{0,240},{8,248},{16,0},{24,8},{32,16},{40,24},{48,32},{56,40},{64,... | collective-permute-start | bytes 4816904 | tf_op jit(solution)/shard_map/ppermute | solution.py:13
  237.4 38.3 %collective-permute-start.6 = (bf16[224,3584]{1,0:T(8,128)(2,1)S(1)}, bf16[224,3584]{1,0:T(8,128)(2,1)S(1)}, u32[]{:S(2)}, u32[]{:S(2)}) collective-permute-start(bf16[224,3584]{1,0:T(8,128)(2,1)S(1)} %get-tuple-element.4), channel_id=1, source_target_pairs={{0,16},{8,24},{16,32},{24,40},{32,48},{40,56},{48,64},{56,72},{64,... | collective-permute-start | bytes 4816904 | tf_op jit(solution)/shard_map/ppermute | solution.py:13
  237.5 68.8 %collective-permute-start.3 = (bf16[224,3584]{1,0:T(8,128)(2,1)S(1)}, bf16[224,3584]{1,0:T(8,128)(2,1)S(1)}, u32[]{:S(2)}, u32[]{:S(2)}) collective-permute-start(bf16[224,3584]{1,0:T(8,128)(2,1)S(1)} %get-tuple-element.5), channel_id=1, source_target_pairs={{0,240},{8,248},{16,0},{24,8},{32,16},{40,24},{48,32},{56,40},{64,... | collective-permute-start | bytes 4816904 | tf_op jit(solution)/shard_map/ppermute | solution.py:13
  241.0 69.1 %collective-permute-start.2 = (bf16[224,3584]{1,0:T(8,128)(2,1)S(1)}, bf16[224,3584]{1,0:T(8,128)(2,1)S(1)}, u32[]{:S(2)}, u32[]{:S(2)}) collective-permute-start(bf16[224,3584]{1,0:T(8,128)(2,1)S(1)} %get-tuple-element.5), channel_id=1, source_target_pairs={{0,16},{8,24},{16,32},{24,40},{32,48},{40,56},{48,64},{56,72},{64,... | collective-permute-start | bytes 4816904 | tf_op jit(solution)/shard_map/ppermute | solution.py:13
Sparse Core Ops, SparseCore 0:
  10.6 172.2 all-gather.1
where the time goes:
time: 321 us
  waiting for transfers between devices  279 us (87%)
  between operations  14.1 us (4%)
  starting transfers between devices  12.2 us (4%)
  matrix products  10.3 us (3%)
  other arithmetic  5.22 us (2%)
    all_gather x1, waiting for transfers between devices, body(): gathered = lax.all_gather(out_grad, 'tensor', axis=1, tiled=True)  175 us
    ppermute x8, waiting for transfers between devices, passed_along(): return lax.ppermute(value, axis, pairs)  103 us
    ppermute x8, starting transfers between devices, passed_along(): return lax.ppermute(value, axis, pairs)  12.2 us
    dot_general x1, matrix products, body(): lax.dot_general(local_ctx, gathered[0], (((0,), (0,)), ((), ())), preferr...  10.3 us
  transfers between devices with their start and end apart: 9, of which 7 were waited for; matrix products, arithmetic and copies ran while one was open for 0% of the time, Pallas kernels for 0%

commit v1 on v0

--- a/solution.py
+++ b/solution.py
@@ -19,7 +19,9 @@
 
 def body(context, out_grad, params, momentum):
     local_ctx = context[0]
-    gathered = lax.all_gather(out_grad, "tensor", axis=1, tiled=True)
+    gathered = jnp.concatenate(
+        lax.all_to_all(jnp.stack([out_grad] * lax.axis_size("tensor")), "tensor", 0, 0), axis=1
+    )
     grad = lax.dot_general(
         local_ctx, gathered[0], (((0,), (0,)), ((), ())), preferred_element_type=jnp.float32
     )

time: 321 us -> 306 us (0.953)
  waiting for transfers between devices: 279 us -> 101 us
  blocking collectives: 0 us -> 169 us
  between operations: 14.1 us -> 0.68 us
  starting transfers between devices: 12.2 us -> 19.3 us
  matrix products: 10.3 us -> 5.3 us
  local copies, waits for them, and re-layouts: 0.01 us -> 3.59 us
    all_gather x1 -> x0, waiting for transfers between devices: 175 us -> none  [body(): gathered = lax.all_gather(out_grad, 'tensor', axis=1, tiled=True)]
    all_to_all x0 -> x1, blocking collectives: none -> 169 us  [body(): lax.all_to_all(jnp.stack([out_grad] * lax.axis_size('tensor')), 'tensor',...]
    ppermute x8, starting transfers between devices: 12.2 us -> 19.3 us  [passed_along(): return lax.ppermute(value, axis, pairs)]
    dot_general x1, matrix products: 10.3 us -> 5.3 us  [body(): lax.dot_general(local_ctx, gathered[0], (((0,), (0,)), ((), ())), preferr...]
    another operation x0 -> x1, local copies, waits for them, and re-layouts: none -> 3.56 us  [body(): jnp.stack([out_grad] * lax.axis_size('tensor'))]
  transfers between devices with their start and end apart: 9 -> 8, of which waited for: 7 -> 6; matrix products, arithmetic and copies ran while one was open for 0% -> 0% of each run, Pallas kernels for 0% -> 0%
where the time goes in v1:
time: 306 us; the launch traced here: 305 us
  blocking collectives  169 us (55%)
  waiting for transfers between devices  101 us (33%)
  starting transfers between devices  19.3 us (6%)
  other arithmetic  6.36 us (2%)
  matrix products  5.3 us (2%)
  local copies, waits for them, and re-layouts  3.59 us (1%)
    all_to_all x1, blocking collectives, body(): lax.all_to_all(jnp.stack([out_grad] * lax.axis_size('tensor')), 'tensor',...  169 us
    ppermute x8, waiting for transfers between devices, passed_along(): return lax.ppermute(value, axis, pairs)  101 us
    ppermute x8, starting transfers between devices, passed_along(): return lax.ppermute(value, axis, pairs)  19.3 us
  transfers between devices with their start and end apart: 8, of which 6 were waited for; matrix products, arithmetic and copies ran while one was open for 0% of the time, Pallas kernels for 0%

profile of v1, /device:TPU:1, one launch (start us, length us, event | category | flops | bytes accessed | tf_op | source)
XLA Modules:
  0.0 305.5 jit_solution(8866834969203136301)
XLA Ops:
  0.6 0.0 copy-start
  0.6 3.6 %stack.2 = bf16[8,1,256,3584]{3,2,1,0:T(8,128)(2,1)S(1)} broadcast(bf16[256,3584]{1,0:T(8,128)(2,1)} %bitcast.25), dimensions={2,3} | broadcast | bytes 16515072 | tf_op jit(solution)/shard_map/stack | solution.py:23
  4.2 0.0 copy-start.1
  4.2 0.0 copy-start.2
  4.2 169.2 %all_to_all.5 = bf16[8,1,256,3584]{3,2,1,0:T(8,128)(2,1)S(1)} all-to-all(bf16[8,1,256,3584]{3,2,1,0:T(8,128)(2,1)S(1)} %stack.2), channel_id=1, replica_groups=mesh['replica'=32,'tensor'=8] {'tensor'}, dimensions={0} | all-to-all | bytes 29360128 | tf_op jit(solution)/shard_map/all_to_all | solution.py:23
  173.4 0.0 copy-done
  173.4 0.0 copy-done.1
  173.4 0.0 copy-done.2
  173.4 5.3 %fusion.5 = (bf16[224,3584]{1,0:T(8,128)(2,1)}, bf16[224,3584]{1,0:T(8,128)(2,1)}, f32[224,3584]{1,0:T(8,128)S(1)}) fusion(f32[1,224,3584]{2,1,0:T(8,128)S(1)} %copy-done.1, bf16[2048,3584]{1,0:T(8,128)(2,1)S(1)} %bitcast.24, bf16[1,2048,224]{1,2,0:T(8,128)(2,1)S(1)} %copy-done, bf16[1,224,3584]{2,1,0:T(8,128)(2,1)S(1)} %copy-done.2), kind=kOutput, calls=%fused_computation.11 | convolution fusion | flops 3293954048 | bytes 26836992 | tf_op jit(solution)/shard_map/dot_general | solution.py:25
  178.7 2.5 collective-permute-start.5
  181.3 1.5 collective-permute-start.4
  182.8 4.3 %collective-permute-start.1 = (bf16[224,3584]{1,0:T(8,128)(2,1)}, bf16[224,3584]{1,0:T(8,128)(2,1)S(1)}, u32[]{:S(2)}, u32[]{:S(2)}) collective-permute-start(bf16[224,3584]{1,0:T(8,128)(2,1)} %get-tuple-element.7), channel_id=1, source_target_pairs={{0,248},{8,0},{16,8},{24,16},{32,24},{40,32},{48,40},{56,48},{64,5... | collective-permute-start | bytes 4816904 | tf_op jit(solution)/shard_map/ppermute | solution.py:13
  187.1 0.0 collective-permute-start
  187.1 14.7 %collective-permute-done.5 = bf16[224,3584]{1,0:T(8,128)(2,1)S(1)} collective-permute-done((bf16[224,3584]{1,0:T(8,128)(2,1)}, bf16[224,3584]{1,0:T(8,128)(2,1)S(1)}, u32[]{:S(2)}, u32[]{:S(2)}) %collective-permute-start.5) | collective-permute-done | bytes 1605664 | tf_op jit(solution)/shard_map/ppermute | solution.py:13
  201.7 0.0 collective-permute-done.4
  201.7 17.2 %collective-permute-done.1 = bf16[224,3584]{1,0:T(8,128)(2,1)S(1)} collective-permute-done((bf16[224,3584]{1,0:T(8,128)(2,1)}, bf16[224,3584]{1,0:T(8,128)(2,1)S(1)}, u32[]{:S(2)}, u32[]{:S(2)}) %collective-permute-start.1) | collective-permute-done | bytes 1605664 | tf_op jit(solution)/shard_map/ppermute | solution.py:13
  218.9 0.0 collective-permute-done
  218.9 2.6 fusion.2
  221.5 7.4 %collective-permute-start.7 = (bf16[224,3584]{1,0:T(8,128)(2,1)}, bf16[224,3584]{1,0:T(8,128)(2,1)S(1)}, u32[]{:S(2)}, u32[]{:S(2)}) collective-permute-start(bf16[224,3584]{1,0:T(8,128)(2,1)} %get-tuple-element.4), channel_id=1, source_target_pairs={{0,240},{8,248},{16,0},{24,8},{32,16},{40,24},{48,32},{56,40},{64,... | collective-permute-start | bytes 4816904 | tf_op jit(solution)/shard_map/ppermute | solution.py:13
  229.0 0.0 collective-permute-start.6
  229.0 3.6 %collective-permute-start.3 = (bf16[224,3584]{1,0:T(8,128)(2,1)S(1)}, bf16[224,3584]{1,0:T(8,128)(2,1)S(1)}, u32[]{:S(2)}, u32[]{:S(2)}) collective-permute-start(bf16[224,3584]{1,0:T(8,128)(2,1)S(1)} %get-tuple-element.5), channel_id=1, source_target_pairs={{0,240},{8,248},{16,0},{24,8},{32,16},{40,24},{48,32},{56,40},{64,... | collective-permute-start | bytes 4816904 | tf_op jit(solution)/shard_map/ppermute | solution.py:13
  232.5 0.0 collective-permute-start.2
  232.6 30.9 %collective-permute-done.7 = bf16[224,3584]{1,0:T(8,128)(2,1)S(1)} collective-permute-done((bf16[224,3584]{1,0:T(8,128)(2,1)}, bf16[224,3584]{1,0:T(8,128)(2,1)S(1)}, u32[]{:S(2)}, u32[]{:S(2)}) %collective-permute-start.7) | collective-permute-done | bytes 1605664 | tf_op jit(solution)/shard_map/ppermute | solution.py:13
  263.4 3.9 %collective-permute-done.6 = bf16[224,3584]{1,0:T(8,128)(2,1)S(1)} collective-permute-done((bf16[224,3584]{1,0:T(8,128)(2,1)}, bf16[224,3584]{1,0:T(8,128)(2,1)S(1)}, u32[]{:S(2)}, u32[]{:S(2)}) %collective-permute-start.6) | collective-permute-done | bytes 1605664 | tf_op jit(solution)/shard_map/ppermute | solution.py:13
  267.3 30.4 %collective-permute-done.3 = bf16[224,3584]{1,0:T(8,128)(2,1)S(1)} collective-permute-done((bf16[224,3584]{1,0:T(8,128)(2,1)S(1)}, bf16[224,3584]{1,0:T(8,128)(2,1)S(1)}, u32[]{:S(2)}, u32[]{:S(2)}) %collective-permute-start.3) | collective-permute-done | bytes 1605664 | tf_op jit(solution)/shard_map/ppermute | solution.py:13
  297.7 4.0 %collective-permute-done.2 = bf16[224,3584]{1,0:T(8,128)(2,1)S(1)} collective-permute-done((bf16[224,3584]{1,0:T(8,128)(2,1)S(1)}, bf16[224,3584]{1,0:T(8,128)(2,1)S(1)}, u32[]{:S(2)}, u32[]{:S(2)}) %collective-permute-start.2) | collective-permute-done | bytes 1605664 | tf_op jit(solution)/shard_map/ppermute | solution.py:13
  301.7 3.8 %fusion = (bf16[1,224,3584]{2,1,0:T(8,128)(2,1)}, f32[1,224,3584]{2,1,0:T(8,128)}) fusion(bf16[224,3584]{1,0:T(8,128)(2,1)S(1)} %collective-permute-done.7, bf16[224,3584]{1,0:T(8,128)(2,1)S(1)} %collective-permute-done.6, bf16[224,3584]{1,0:T(8,128)(2,1)S(1)} %collective-permute-done.5, f32[224,3584]{1,0:T(8,128)S(1)} %get-tuple-element.8, ...), kind=kLoop, calls=%fused_computation.6 | loop fusion | flops 18464768 | bytes 24084480 | tf_op jit(solution)/shard_map/broadcast_in_dim | solution.py:42
Async XLA Ops:
  0.6 172.8 %copy-start = (bf16[1,2048,224]{1,2,0:T(8,128)(2,1)S(1)}, bf16[1,2048,224]{1,2,0:T(8,128)(2,1)}, u32[]{:S(2)}) copy-start(bf16[1,2048,224]{1,2,0:T(8,128)(2,1)} %param.4) | copy-start | bytes 2752516
  4.2 169.2 %copy-start.1 = (f32[1,224,3584]{2,1,0:T(8,128)S(1)}, f32[1,224,3584]{2,1,0:T(8,128)}, u32[]{:S(2)}) copy-start(f32[1,224,3584]{2,1,0:T(8,128)} %param.6) | copy-start | bytes 9633796
  4.2 169.2 %copy-start.2 = (bf16[1,224,3584]{2,1,0:T(8,128)(2,1)S(1)}, bf16[1,224,3584]{2,1,0:T(8,128)(2,1)}, u32[]{:S(2)}) copy-start(bf16[1,224,3584]{2,1,0:T(8,128)(2,1)} %param.7) | copy-start | bytes 4816900
  178.7 23.0 %collective-permute-start.5 = (bf16[224,3584]{1,0:T(8,128)(2,1)}, bf16[224,3584]{1,0:T(8,128)(2,1)S(1)}, u32[]{:S(2)}, u32[]{:S(2)}) collective-permute-start(bf16[224,3584]{1,0:T(8,128)(2,1)} %get-tuple-element.6), channel_id=1, source_target_pairs={{0,248},{8,0},{16,8},{24,16},{32,24},{40,32},{48,40},{56,48},{64,5... | collective-permute-start | bytes 4816904 | tf_op jit(solution)/shard_map/ppermute | solution.py:13
  181.3 20.5 %collective-permute-start.4 = (bf16[224,3584]{1,0:T(8,128)(2,1)}, bf16[224,3584]{1,0:T(8,128)(2,1)S(1)}, u32[]{:S(2)}, u32[]{:S(2)}) collective-permute-start(bf16[224,3584]{1,0:T(8,128)(2,1)} %get-tuple-element.6), channel_id=1, source_target_pairs={{0,8},{8,16},{16,24},{24,32},{32,40},{40,48},{48,56},{56,64},{64,7... | collective-permute-start | bytes 4816904 | tf_op jit(solution)/shard_map/ppermute | solution.py:13
  182.8 36.2 %collective-permute-start.1 = (bf16[224,3584]{1,0:T(8,128)(2,1)}, bf16[224,3584]{1,0:T(8,128)(2,1)S(1)}, u32[]{:S(2)}, u32[]{:S(2)}) collective-permute-start(bf16[224,3584]{1,0:T(8,128)(2,1)} %get-tuple-element.7), channel_id=1, source_target_pairs={{0,248},{8,0},{16,8},{24,16},{32,24},{40,32},{48,40},{56,48},{64,5... | collective-permute-start | bytes 4816904 | tf_op jit(solution)/shard_map/ppermute | solution.py:13
  187.1 31.9 %collective-permute-start = (bf16[224,3584]{1,0:T(8,128)(2,1)}, bf16[224,3584]{1,0:T(8,128)(2,1)S(1)}, u32[]{:S(2)}, u32[]{:S(2)}) collective-permute-start(bf16[224,3584]{1,0:T(8,128)(2,1)} %get-tuple-element.7), channel_id=1, source_target_pairs={{0,8},{8,16},{16,24},{24,32},{32,40},{40,48},{48,56},{56,64},{64,7... | collective-permute-start | bytes 4816904 | tf_op jit(solution)/shard_map/ppermute | solution.py:13
  221.5 41.9 %collective-permute-start.7 = (bf16[224,3584]{1,0:T(8,128)(2,1)}, bf16[224,3584]{1,0:T(8,128)(2,1)S(1)}, u32[]{:S(2)}, u32[]{:S(2)}) collective-permute-start(bf16[224,3584]{1,0:T(8,128)(2,1)} %get-tuple-element.4), channel_id=1, source_target_pairs={{0,240},{8,248},{16,0},{24,8},{32,16},{40,24},{48,32},{56,40},{64,... | collective-permute-start | bytes 4816904 | tf_op jit(solution)/shard_map/ppermute | solution.py:13
  229.0 38.3 %collective-permute-start.6 = (bf16[224,3584]{1,0:T(8,128)(2,1)}, bf16[224,3584]{1,0:T(8,128)(2,1)S(1)}, u32[]{:S(2)}, u32[]{:S(2)}) collective-permute-start(bf16[224,3584]{1,0:T(8,128)(2,1)} %get-tuple-element.4), channel_id=1, source_target_pairs={{0,16},{8,24},{16,32},{24,40},{32,48},{40,56},{48,64},{56,72},{64,... | collective-permute-start | bytes 4816904 | tf_op jit(solution)/shard_map/ppermute | solution.py:13
  229.0 68.7 %collective-permute-start.3 = (bf16[224,3584]{1,0:T(8,128)(2,1)S(1)}, bf16[224,3584]{1,0:T(8,128)(2,1)S(1)}, u32[]{:S(2)}, u32[]{:S(2)}) collective-permute-start(bf16[224,3584]{1,0:T(8,128)(2,1)S(1)} %get-tuple-element.5), channel_id=1, source_target_pairs={{0,240},{8,248},{16,0},{24,8},{32,16},{40,24},{48,32},{56,40},{64,... | collective-permute-start | bytes 4816904 | tf_op jit(solution)/shard_map/ppermute | solution.py:13
  232.5 69.2 %collective-permute-start.2 = (bf16[224,3584]{1,0:T(8,128)(2,1)S(1)}, bf16[224,3584]{1,0:T(8,128)(2,1)S(1)}, u32[]{:S(2)}, u32[]{:S(2)}) collective-permute-start(bf16[224,3584]{1,0:T(8,128)(2,1)S(1)} %get-tuple-element.5), channel_id=1, source_target_pairs={{0,16},{8,24},{16,32},{24,40},{32,48},{40,56},{48,64},{56,72},{64,... | collective-permute-start | bytes 4816904 | tf_op jit(solution)/shard_map/ppermute | solution.py:13
